TPU v7x, 768 devices: a whole 4x8x12 slice. The times are simulated.
768 devices in a mesh: row: 96 (over y_lo, z, x), col: 8 (over y_hi, core).
Axes of the slice: x: 4, y: 8 (y_hi: 4, y_lo: 2; y = y_hi * 2 + y_lo), z: 12, core: 2. Of those that a mesh axis runs over, the one named last changes fastest.
Arguments:
- momentum: bfloat16 [24576, 3072], P('row', 'col'), may hold values from -0.125 to 0.125
Outputs:
- update: bfloat16 [24576, 3072], P('row', 'col')
All inputs are finite; a program needn't handle non-finite values.
Results may differ from a plain program's by a relative error of at most 0.0084.
Values may be sent and summed in bfloat16 or wider, within the bound.
No kernel may reach another device: no remote copies, remote signals or barrier semaphores. Data moves between devices by JAX's collectives and lax.ppermute only.
A program may use at most 32 MiB of HBM per device.

v0:
```python
import math

import jax
import jax.numpy as jnp
from jax import lax
from jax.sharding import PartitionSpec as P

coef_first = 3.4445
coef_middle = -4.775
coef_last = 2.0315


def body(momentum):
    row_panel = lax.all_gather(momentum, "col", axis=1, tiled=True)
    width = row_panel.shape[1]
    total_rows = momentum.shape[0] * lax.axis_size("row")
    gram_piece = lax.psum_scatter(
        lax.dot_general(
            row_panel, momentum, (((0,), (0,)), ((), ())), preferred_element_type=jnp.float32
        ),
        "row",
        scatter_dimension=0,
        tiled=True,
    )
    gram_block = lax.all_gather(gram_piece.astype(jnp.bfloat16), "row", axis=0, tiled=True)

    def times_gram(left):
        return jnp.dot(left, gram_block, preferred_element_type=jnp.float32)

    mixed = times_gram(row_panel).astype(jnp.bfloat16)
    mixed_panel = lax.all_gather(mixed, "col", axis=1, tiled=True)
    second = times_gram(mixed_panel)
    rms_scale = 0.2 * math.sqrt(max(total_rows, width))
    total = (
        coef_first * momentum.astype(jnp.float32)
        + coef_middle * mixed.astype(jnp.float32)
        + coef_last * second
    )
    return (rms_scale * total).astype(jnp.bfloat16)


def solution(mesh):
    return jax.shard_map(
        body,
        mesh=mesh,
        in_specs=(P("row", "col"),),
        out_specs=P("row", "col"),
        check_vma=False,
    )
```

profile of v0, /device:TPU:1, one launch (start us, length us, event | category | flops | bytes accessed | tf_op | source)
XLA Modules:
  0.0 1030.1 jit_solution(9673290761813248480)
XLA Ops:
  6.5 0.0 all-gather.4.cloned.1.call-start
  6.5 0.7 all-gather.4.cloned.1.call-update
  7.3 0.0 reduce-scatter.2.cloned.1.call-start
  7.3 49.0 %all-gather.4.cloned.1.call-done = bf16[256,3072]{1,0:T(8,128)(2,1)} async-done(((bf16[256,384]{1,0:T(8,128)(2,1)}), bf16[256,3072]{1,0:T(8,128)(2,1)}) %all-gather.4.cloned.1.call-update) | async-done | bytes 1572880 | tf_op jit(solution)/shard_map/all_gather | solution.py:14
  56.4 4.6 fusion.4
  60.9 0.0 copy-start
  60.9 0.0 reduce-scatter.2.cloned.1.call-update
  60.9 0.0 all-gather.6.cloned.1.call-start
  61.0 403.3 %reduce-scatter.2.cloned.1.call-done = f32[32,384]{1,0:T(8,128)} async-done(((f32[3072,384]{1,0:T(8,128)}), f32[32,384]{1,0:T(8,128)}) %reduce-scatter.2.cloned.1.call-update) | async-done | bytes 49168 | tf_op jit(solution)/shard_map/reduce_scatter | solution.py:17
  464.3 1.4 convert_element_type.19
  465.7 0.0 all-gather.6.cloned.1.call-update
  465.7 0.0 copy-start.1
  465.7 0.0 all-gather.8.cloned.1.call-start
  465.8 453.7 %all-gather.6.cloned.1.call-done = bf16[3072,384]{1,0:T(8,128)(2,1)} async-done(((bf16[32,384]{1,0:T(8,128)(2,1)}), bf16[3072,384]{1,0:T(8,128)(2,1)}) %all-gather.6.cloned.1.call-update) | async-done | bytes 2359312 | tf_op jit(solution)/shard_map/all_gather | solution.py:25
  919.5 0.0 copy-done
  919.5 3.2 fusion.3
  922.7 0.0 all-gather.8.cloned.1.call-update
  922.7 0.0 copy-done.1
  922.7 0.1 copy.2
  922.9 96.7 %all-gather.8.cloned.1.call-done = bf16[256,3072]{0,1:T(8,128)(2,1)} async-done(((bf16[256,384]{0,1:T(8,128)(2,1)}), bf16[256,3072]{0,1:T(8,128)(2,1)}) %all-gather.8.cloned.1.call-update) | async-done | bytes 1572880 | tf_op jit(solution)/shard_map/all_gather | solution.py:31
  1019.6 3.2 fusion.2
  1022.7 0.8 copy.4
Async XLA Ops:
  6.5 49.8 %all-gather.4.cloned.1.call-start = ((), (), s32[]{:S(2)}) async-start(), calls=%async_computation.1 | async-start | bytes 1769472 | tf_op jit(solution)/shard_map/all_gather | solution.py:14
  7.3 457.0 %reduce-scatter.2.cloned.1.call-start = ((), (), s32[]{:S(2)}) async-start(), calls=%async_computation.2 | async-start | bytes 4767744 | tf_op jit(solution)/shard_map/reduce_scatter | solution.py:17
  60.9 858.6 %copy-start = (bf16[256,3072]{1,0:T(8,128)(2,1)S(1)}, bf16[256,3072]{1,0:T(8,128)(2,1)}, u32[]{:S(2)}) copy-start(bf16[256,3072]{1,0:T(8,128)(2,1)} %all-gather.4.cloned.1.call-done) | copy-start | bytes 4718596
  60.9 858.6 %all-gather.6.cloned.1.call-start = ((), (), s32[]{:S(2)}) async-start(), calls=%async_computation.3 | async-start | bytes 2383872 | tf_op jit(solution)/shard_map/all_gather | solution.py:25
  465.7 457.0 %copy-start.1 = (bf16[256,384]{1,0:T(8,128)(2,1)S(1)}, bf16[256,384]{1,0:T(8,128)(2,1)}, u32[]{:S(2)}) copy-start(bf16[256,384]{1,0:T(8,128)(2,1)} %param.1) | copy-start | bytes 589828
  465.7 553.9 %all-gather.8.cloned.1.call-start = ((), (), s32[]{:S(2)}) async-start(), calls=%async_computation.4 | async-start | bytes 1769472 | tf_op jit(solution)/shard_map/all_gather | solution.py:31
Sparse Core Ops, SparseCore 0:
  9.8 46.5 all-gather.3
  61.1 403.1 reduce-scatter.1
  466.9 452.5 all-gather.5
  922.8 96.7 all-gather.7
where the time goes:
time: 1030 us
  waiting for transfers between devices  1000 us (97%)
  between operations  13.2 us (1%)
  matrix products  10.9 us (1%)
    all_gather x1, waiting for transfers between devices, body(): lax.all_gather(gram_piece.astype(jnp.bfloat16), 'row', axis=0, tiled=True)  454 us
    reduce_scatter x1, waiting for transfers between devices, body(): lax.psum_scatter(lax.dot_general(row_panel, momentum, (((0,), (0,)), ((),...  403 us
    all_gather x1, waiting for transfers between devices, body(): mixed_panel = lax.all_gather(mixed, 'col', axis=1, tiled=True)  96.7 us
    all_gather x1, waiting for transfers between devices, body(): row_panel = lax.all_gather(momentum, 'col', axis=1, tiled=True)  49 us
  transfers between devices with their start and end apart: 4, of which 4 were waited for; matrix products, arithmetic and copies ran while one was open for 0% of the time, Pallas kernels for 0%

commit v1 on v0

v1 whole, which is shorter than its diff:
```python
import math

import jax
import jax.numpy as jnp
from jax import lax
from jax.sharding import Mesh
from jax.sharding import PartitionSpec as P

coef_first = 3.4445
coef_middle = -4.775
coef_last = 2.0315

axes = ("yl", "z", "x", "yh", "core")
row_axes = ("yl", "z", "x")
col_axes = ("yh", "core")
axis_sizes = (2, 12, 4, 4, 2)


def spread(block, names, count):
    copies = jnp.broadcast_to(block[None], (count,) + block.shape)
    return lax.all_to_all(copies, names, 0, 0, tiled=True)


def gather_columns(block):
    near = spread(block, "yh", 4)
    far = lax.ppermute(near, "core", [(0, 1), (1, 0)])
    return jnp.concatenate([near, far], axis=0)


def body(momentum):
    with jax.named_scope("panel"):
        panel = gather_columns(momentum)
    with jax.named_scope("gram"):
        partial = lax.dot_general(
            panel, momentum, (((1,), (0,)), ((), ())), preferred_element_type=jnp.float32
        ).astype(jnp.bfloat16)
    with jax.named_scope("reduce"):
        parts = lax.all_to_all(partial, ("yl", "x"), 0, 0, tiled=True)
        block = jnp.sum(parts.astype(jnp.float32), axis=0).astype(jnp.bfloat16)
        parts = lax.all_to_all(block.reshape(12, 32, 384), "z", 0, 0, tiled=True)
        piece = jnp.sum(parts.astype(jnp.float32), axis=0).astype(jnp.bfloat16)
    with jax.named_scope("collect"):
        block = spread(piece, "z", 12).reshape(384, 384)
        gram = spread(block, ("yl", "x"), 8)

    def times_gram(left):
        return lax.dot_general(
            left, gram, (((0, 2), (0, 1)), ((), ())), preferred_element_type=jnp.float32
        )

    with jax.named_scope("mixed"):
        mixed = times_gram(panel).astype(jnp.bfloat16)
    with jax.named_scope("mixed_panel"):
        mixed_panel = gather_columns(mixed)
    with jax.named_scope("second"):
        second = times_gram(mixed_panel)
        rms_scale = 0.2 * math.sqrt(max(momentum.shape[0] * 96, 3072))
        total = (
            coef_first * momentum.astype(jnp.float32)
            + coef_middle * mixed.astype(jnp.float32)
            + coef_last * second
        )
        return (rms_scale * total).astype(jnp.bfloat16)


def solution(mesh):
    fine = Mesh(mesh.devices.reshape(axis_sizes), axes)
    return jax.shard_map(
        body,
        mesh=fine,
        in_specs=(P(row_axes, col_axes),),
        out_specs=P(row_axes, col_axes),
        check_vma=False,
    )
```

time: 1030 us -> 185 us (0.18)
  the two profiles are of different devices: /device:TPU:1 before, /device:TPU:65 now
where the time goes in v1:
time: 185 us; the launch traced here: 184 us
  blocking collectives  166 us (90%)
  starting transfers between devices  8.32 us (4%)
  waiting for transfers between devices  3.72 us (2%)
  matrix products  3.66 us (2%)
    all_to_all x4, blocking collectives, spread(): return lax.all_to_all(copies, names, 0, 0, tiled=True)  104 us
    all_to_all x1, blocking collectives, body(): parts = lax.all_to_all(partial, ('yl', 'x'), 0, 0, tiled=True)  32.3 us
    all_to_all x1, blocking collectives, body(): parts = lax.all_to_all(block.reshape(12, 32, 384), 'z', 0, 0, tiled=True)  30 us
    ppermute x2, starting transfers between devices, gather_columns(): far = lax.ppermute(near, 'core', [(0, 1), (1, 0)])  8.32 us
    ppermute x2, waiting for transfers between devices, gather_columns(): far = lax.ppermute(near, 'core', [(0, 1), (1, 0)])  3.72 us
  transfers between devices with their start and end apart: 2, of which 2 were waited for; matrix products, arithmetic and copies ran while one was open for 0% of the time, Pallas kernels for 0%

profile of v1, /device:TPU:65, one launch (start us, length us, event | category | flops | bytes accessed | tf_op | source)
XLA Modules:
  0.0 184.3 jit_solution(16490010446665760339)
XLA Ops:
  0.0 1.1 copy.4
  1.1 0.1 broadcast_in_dim.10
  1.1 27.4 %all_to_all.30 = bf16[4,256,384]{1,2,0:T(8,128)(2,1)S(1)} all-to-all(bf16[4,256,384]{1,2,0:T(8,128)(2,1)S(1)} %broadcast_in_dim.10), channel_id=1, replica_groups=mesh['yl'=2,'z'=12,'x'=4,'yh'=4,'core'=2] {'yh'}, dimensions={0} | all-to-all | bytes 1572864 | tf_op jit(solution)/shard_map/panel/all_to_all | solution.py:21
  28.5 0.0 copy-start.2
  28.5 4.2 %collective-permute-start = (bf16[4,256,384]{1,2,0:T(8,128)(2,1)S(1)}, bf16[4,256,384]{1,2,0:T(8,128)(2,1)S(1)}, u32[]{:S(2)}, u32[]{:S(2)}) collective-permute-start(bf16[4,256,384]{1,2,0:T(8,128)(2,1)S(1)} %all_to_all.30), channel_id=1, source_target_pairs={{0,1},{1,0},{2,3},{3,2},{4,5},{5,4},{6,7},{7,6},{8,9},{9,8},{10,11... | collective-permute-start | bytes 2359304 | tf_op jit(solution)/shard_map/panel/ppermute | solution.py:26
  32.7 0.1 constant_dynamic-update-slice_fusion.1
  32.8 1.8 collective-permute-done
  34.6 0.1 constant_dynamic-update-slice_fusion
  34.7 0.0 copy-done.2
  34.7 0.0 copy-start
  34.7 1.0 convolution_convert_fusion
  35.7 0.2 copy-done
  35.8 32.3 %all_to_all.31 = bf16[8,384,384]{2,1,0:T(8,128)(2,1)S(1)} all-to-all(bf16[8,384,384]{2,1,0:T(8,128)(2,1)S(1)} %convolution_convert_fusion), channel_id=1, replica_groups=mesh['yl'=2,'z'=12,'x'=4,'yh'=4,'core'=2] {'yl','x'}, dimensions={0} | all-to-all | bytes 4718592 | tf_op jit(solution)/shard_map/reduce/all_to_all | solution.py:38
  68.1 0.5 reduce_sum.24
  68.6 30.0 %all_to_all.32 = bf16[12,32,384]{2,1,0:T(8,128)(2,1)S(1)} all-to-all(bf16[12,32,384]{2,1,0:T(8,128)(2,1)S(1)} %bitcast.23), channel_id=1, replica_groups=mesh['yl'=2,'z'=12,'x'=4,'yh'=4,'core'=2] {'z'}, dimensions={0} | all-to-all | bytes 589824 | tf_op jit(solution)/shard_map/reduce/all_to_all | solution.py:40
  98.7 18.5 %all_to_all.33 = bf16[12,32,384]{2,1,0:T(8,128)(2,1)S(1)} all-to-all(bf16[12,32,384]{2,1,0:T(8,128)(2,1)S(1)} %broadcast_in_dim.11), channel_id=1, replica_groups=mesh['yl'=2,'z'=12,'x'=4,'yh'=4,'core'=2] {'z'}, dimensions={0} | all-to-all | bytes 589824 | tf_op jit(solution)/shard_map/collect/all_to_all | solution.py:21
  117.2 0.2 broadcast_in_dim.13
  117.4 0.0 copy-start.1
  117.4 34.9 %all_to_all.34 = bf16[8,384,384]{2,1,0:T(8,128)(2,1)S(1)} all-to-all(bf16[8,384,384]{2,1,0:T(8,128)(2,1)S(1)} %broadcast_in_dim.13), channel_id=1, replica_groups=mesh['yl'=2,'z'=12,'x'=4,'yh'=4,'core'=2] {'yl','x'}, dimensions={0} | all-to-all | bytes 4718592 | tf_op jit(solution)/shard_map/collect/all_to_all | solution.py:21
  152.4 0.0 copy-done.1
  152.4 1.0 fusion.19
  153.4 0.1 broadcast_in_dim.14
  153.5 23.1 %all_to_all.35 = bf16[4,256,384]{2,1,0:T(8,128)(2,1)S(1)} all-to-all(bf16[4,256,384]{2,1,0:T(8,128)(2,1)S(1)} %broadcast_in_dim.14), channel_id=1, replica_groups=mesh['yl'=2,'z'=12,'x'=4,'yh'=4,'core'=2] {'yh'}, dimensions={0} | all-to-all | bytes 1572864 | tf_op jit(solution)/shard_map/mixed_panel/all_to_all | solution.py:21
  176.6 4.1 %collective-permute-start.1 = (bf16[4,256,384]{2,1,0:T(8,128)(2,1)S(1)}, bf16[4,256,384]{2,1,0:T(8,128)(2,1)S(1)}, u32[]{:S(2)}, u32[]{:S(2)}) collective-permute-start(bf16[4,256,384]{2,1,0:T(8,128)(2,1)S(1)} %all_to_all.35), channel_id=1, source_target_pairs={{0,1},{1,0},{2,3},{3,2},{4,5},{5,4},{6,7},{7,6},{8,9},{9,8},{10,11... | collective-permute-start | bytes 2359304 | tf_op jit(solution)/shard_map/mixed_panel/ppermute | solution.py:26
  180.8 1.9 %collective-permute-done.1 = bf16[4,256,384]{2,1,0:T(8,128)(2,1)S(1)} collective-permute-done((bf16[4,256,384]{2,1,0:T(8,128)(2,1)S(1)}, bf16[4,256,384]{2,1,0:T(8,128)(2,1)S(1)}, u32[]{:S(2)}, u32[]{:S(2)}) %collective-permute-start.1) | collective-permute-done | bytes 786464 | tf_op jit(solution)/shard_map/mixed_panel/ppermute | solution.py:26
  182.7 1.7 fusion.16
  (2 shorter events, 0.1 us)
Async XLA Ops:
  28.5 6.1 %copy-start.2 = (bf16[256,384]{1,0:T(8,128)(2,1)S(1)}, bf16[256,384]{1,0:T(8,128)(2,1)}, u32[]{:S(2)}) copy-start(bf16[256,384]{1,0:T(8,128)(2,1)} %param.1) | copy-start | bytes 589828
  28.5 6.1 %collective-permute-start = (bf16[4,256,384]{1,2,0:T(8,128)(2,1)S(1)}, bf16[4,256,384]{1,2,0:T(8,128)(2,1)S(1)}, u32[]{:S(2)}, u32[]{:S(2)}) collective-permute-start(bf16[4,256,384]{1,2,0:T(8,128)(2,1)S(1)} %all_to_all.30), channel_id=1, source_target_pairs={{0,1},{1,0},{2,3},{3,2},{4,5},{5,4},{6,7},{7,6},{8,9},{9,8},{10,11... | collective-permute-start | bytes 2359304 | tf_op jit(solution)/shard_map/panel/ppermute | solution.py:26
  34.7 1.2 copy-start
  117.4 34.9 %copy-start.1 = (bf16[8,256,384]{1,2,0:T(8,128)(2,1)S(1)}, bf16[8,256,384]{1,2,0:T(8,128)(2,1)}, u32[]{:S(2)}) copy-start(bf16[8,256,384]{1,2,0:T(8,128)(2,1)} %copy-done) | copy-start | bytes 4718596
  176.6 6.0 %collective-permute-start.1 = (bf16[4,256,384]{2,1,0:T(8,128)(2,1)S(1)}, bf16[4,256,384]{2,1,0:T(8,128)(2,1)S(1)}, u32[]{:S(2)}, u32[]{:S(2)}) collective-permute-start(bf16[4,256,384]{2,1,0:T(8,128)(2,1)S(1)} %all_to_all.35), channel_id=1, source_target_pairs={{0,1},{1,0},{2,3},{3,2},{4,5},{5,4},{6,7},{7,6},{8,9},{9,8},{10,11... | collective-permute-start | bytes 2359304 | tf_op jit(solution)/shard_map/mixed_panel/ppermute | solution.py:26

commit v2 on v1

v2 whole, which is shorter than its diff:
```python
import math

import jax
import jax.numpy as jnp
from jax import lax
from jax.sharding import Mesh
from jax.sharding import PartitionSpec as P

coef_first = 3.4445
coef_middle = -4.775
coef_last = 2.0315

axes = ("yl", "z", "x", "yh", "core")
row_axes = ("yl", "z", "x")
col_axes = ("yh", "core")
axis_sizes = (2, 12, 4, 4, 2)
chunks = ((0, 384),)


def exchange(blocks, names):
    return lax.all_to_all(blocks, names, 0, 0, tiled=True)


def spread(block, names, count):
    return exchange(jnp.broadcast_to(block[None], (count,) + block.shape), names)


def add_up(parts):
    return jnp.sum(parts.astype(jnp.float32), axis=0).astype(jnp.bfloat16)


def gather_columns(block):
    near = lax.all_gather(block, "yh", axis=0)
    far = lax.ppermute(near, "core", [(0, 1), (1, 0)])
    return jnp.concatenate([near, far], axis=0)


def times(left, right):
    return lax.dot_general(
        left, right, (((0, 2), (0, 1)), ((), ())), preferred_element_type=jnp.float32
    )


def body(momentum):
    with jax.named_scope("panel"):
        panel = gather_columns(momentum)
    grams = []
    for start, stop in chunks:
        width = stop - start
        with jax.named_scope("gram"):
            partial = lax.dot_general(
                panel,
                momentum[:, start:stop],
                (((1,), (0,)), ((), ())),
                preferred_element_type=jnp.float32,
            ).astype(jnp.bfloat16)
        with jax.named_scope("reduce"):
            block = add_up(exchange(partial, ("yl", "x")))
            piece = add_up(exchange(block.reshape(12, 32, width), "z"))
        with jax.named_scope("collect"):
            block = spread(piece, "z", 12).reshape(384, width)
            grams.append(spread(block, ("yl", "x"), 8))
    with jax.named_scope("mixed"):
        mixed = [times(panel, gram).astype(jnp.bfloat16) for gram in grams]
    with jax.named_scope("mixed_panel"):
        mixed_panels = [gather_columns(part) for part in mixed]
    with jax.named_scope("second"):
        gram = jnp.concatenate(grams, axis=2)
        second = sum(
            times(part, gram[:, start:stop])
            for part, (start, stop) in zip(mixed_panels, chunks)
        )
        rms_scale = 0.2 * math.sqrt(max(momentum.shape[0] * 96, 3072))
        total = (
            coef_first * momentum.astype(jnp.float32)
            + coef_middle * jnp.concatenate(mixed, axis=1).astype(jnp.float32)
            + coef_last * second
        )
        return (rms_scale * total).astype(jnp.bfloat16)


def solution(mesh):
    fine = Mesh(mesh.devices.reshape(axis_sizes), axes)
    return jax.shard_map(
        body,
        mesh=fine,
        in_specs=(P(row_axes, col_axes),),
        out_specs=P(row_axes, col_axes),
        check_vma=False,
    )
```

time: 185 us -> 174 us (0.941)
  blocking collectives: 166 us -> 150 us
  starting transfers between devices: 8.32 us -> 14.2 us
    all_to_all x6 -> x4, blocking collectives: 166 us -> 116 us  [exchange(): return lax.all_to_all(blocks, names, 0, 0, tiled=True)]
    all_gather x0 -> x2, blocking collectives: none -> 34.7 us  [gather_columns(): near = lax.all_gather(block, 'yh', axis=0)]
    ppermute x2, starting transfers between devices: 8.32 us -> 14.2 us  [gather_columns(): far = lax.ppermute(near, 'core', [(0, 1), (1, 0)])]
where the time goes in v2:
time: 174 us; the launch traced here: 173 us
  blocking collectives  150 us (86%)
  starting transfers between devices  14.2 us (8%)
  waiting for transfers between devices  3.78 us (2%)
  matrix products  3.7 us (2%)
    all_to_all x4, blocking collectives, exchange(): return lax.all_to_all(blocks, names, 0, 0, tiled=True)  116 us
    all_gather x2, blocking collectives, gather_columns(): near = lax.all_gather(block, 'yh', axis=0)  34.7 us
    ppermute x2, starting transfers between devices, gather_columns(): far = lax.ppermute(near, 'core', [(0, 1), (1, 0)])  14.2 us
    ppermute x2, waiting for transfers between devices, gather_columns(): far = lax.ppermute(near, 'core', [(0, 1), (1, 0)])  3.78 us
  transfers between devices with their start and end apart: 2, of which 2 were waited for; matrix products, arithmetic and copies ran while one was open for 0% of the time, Pallas kernels for 0%

profile of v2, /device:TPU:65, one launch (start us, length us, event | category | flops | bytes accessed | tf_op | source)
XLA Modules:
  0.0 173.2 jit_solution(3529425095271838424)
XLA Ops:
  0.0 0.0 copy-start
  0.0 18.7 %all-gather = bf16[1024,384]{1,0:T(8,128)(2,1)S(1)} all-gather(bf16[256,384]{1,0:T(8,128)(2,1)} %param.1), channel_id=2, replica_groups=mesh['yl'=2,'z'=12,'x'=4,'yh'=4,'core'=2] {'yh'}, dimensions={0}, use_global_device_ids=true | all-gather | bytes 983040 | tf_op jit(solution)/shard_map/panel/all_gather | solution.py:33
  18.7 0.3 copy.7
  19.0 6.7 %collective-permute-start = (bf16[4,256,384]{1,2,0:T(8,128)(2,1)S(1)}, bf16[4,256,384]{1,2,0:T(8,128)(2,1)S(1)}, u32[]{:S(2)}, u32[]{:S(2)}) collective-permute-start(bf16[4,256,384]{1,2,0:T(8,128)(2,1)S(1)} %copy.7), channel_id=1, source_target_pairs={{0,1},{1,0},{2,3},{3,2},{4,5},{5,4},{6,7},{7,6},{8,9},{9,8},{10,11... | collective-permute-start | bytes 2359304 | tf_op jit(solution)/shard_map/panel/ppermute | solution.py:34
  25.7 1.9 %collective-permute-done = bf16[4,256,384]{1,2,0:T(8,128)(2,1)S(1)} collective-permute-done((bf16[4,256,384]{1,2,0:T(8,128)(2,1)S(1)}, bf16[4,256,384]{1,2,0:T(8,128)(2,1)S(1)}, u32[]{:S(2)}, u32[]{:S(2)}) %collective-permute-start) | collective-permute-done | bytes 786464 | tf_op jit(solution)/shard_map/panel/ppermute | solution.py:34
  27.6 0.0 copy-done
  27.6 0.0 copy-start.2
  27.6 1.0 convolution_convert_fusion
  28.6 0.0 copy-done.2
  28.6 32.3 %all_to_all.20 = bf16[8,384,384]{2,1,0:T(8,128)(2,1)S(1)} all-to-all(bf16[8,384,384]{2,1,0:T(8,128)(2,1)S(1)} %convolution_convert_fusion), channel_id=1, replica_groups=mesh['yl'=2,'z'=12,'x'=4,'yh'=4,'core'=2] {'yl','x'}, dimensions={0} | all-to-all | bytes 4718592 | tf_op jit(solution)/shard_map/reduce/all_to_all | solution.py:21
  60.9 0.5 reduce_sum.24
  61.4 30.1 %all_to_all.21 = bf16[12,32,384]{2,1,0:T(8,128)(2,1)S(1)} all-to-all(bf16[12,32,384]{2,1,0:T(8,128)(2,1)S(1)} %bitcast.24), channel_id=1, replica_groups=mesh['yl'=2,'z'=12,'x'=4,'yh'=4,'core'=2] {'z'}, dimensions={0} | all-to-all | bytes 589824 | tf_op jit(solution)/shard_map/reduce/all_to_all | solution.py:21
  91.5 18.5 %all_to_all.22 = bf16[12,32,384]{2,1,0:T(8,128)(2,1)S(1)} all-to-all(bf16[12,32,384]{2,1,0:T(8,128)(2,1)S(1)} %broadcast_in_dim.6), channel_id=1, replica_groups=mesh['yl'=2,'z'=12,'x'=4,'yh'=4,'core'=2] {'z'}, dimensions={0} | all-to-all | bytes 589824 | tf_op jit(solution)/shard_map/collect/all_to_all | solution.py:21
  110.0 0.2 broadcast_in_dim.15
  110.3 0.0 copy-start.3
  110.3 34.9 %all_to_all.23 = bf16[8,384,384]{2,1,0:T(8,128)(2,1)S(1)} all-to-all(bf16[8,384,384]{2,1,0:T(8,128)(2,1)S(1)} %broadcast_in_dim.15), channel_id=1, replica_groups=mesh['yl'=2,'z'=12,'x'=4,'yh'=4,'core'=2] {'yl','x'}, dimensions={0} | all-to-all | bytes 4718592 | tf_op jit(solution)/shard_map/collect/all_to_all | solution.py:21
  145.2 0.0 copy-done.3
  145.2 0.0 copy-start.1
  145.2 1.0 fusion.19
  146.2 16.0 %all-gather.1 = bf16[1024,384]{1,0:T(8,128)(2,1)S(1)} all-gather(bf16[256,384]{1,0:T(8,128)(2,1)S(1)} %fusion.19), channel_id=3, replica_groups=mesh['yl'=2,'z'=12,'x'=4,'yh'=4,'core'=2] {'yh'}, dimensions={0}, use_global_device_ids=true | all-gather | bytes 983040 | tf_op jit(solution)/shard_map/mixed_panel/all_gather | solution.py:33
  162.2 7.4 %collective-permute-start.1 = (bf16[4,256,384]{2,1,0:T(8,128)(2,1)S(1)}, bf16[4,256,384]{2,1,0:T(8,128)(2,1)S(1)}, u32[]{:S(2)}, u32[]{:S(2)}) collective-permute-start(bf16[4,256,384]{2,1,0:T(8,128)(2,1)S(1)} %bitcast.26), channel_id=1, source_target_pairs={{0,1},{1,0},{2,3},{3,2},{4,5},{5,4},{6,7},{7,6},{8,9},{9,8},{10,11... | collective-permute-start | bytes 2359304 | tf_op jit(solution)/shard_map/mixed_panel/ppermute | solution.py:34
  169.7 1.9 %collective-permute-done.1 = bf16[4,256,384]{2,1,0:T(8,128)(2,1)S(1)} collective-permute-done((bf16[4,256,384]{2,1,0:T(8,128)(2,1)S(1)}, bf16[4,256,384]{2,1,0:T(8,128)(2,1)S(1)}, u32[]{:S(2)}, u32[]{:S(2)}) %collective-permute-start.1) | collective-permute-done | bytes 786464 | tf_op jit(solution)/shard_map/mixed_panel/ppermute | solution.py:34
  171.6 0.0 copy-done.1
  171.6 1.7 fusion.16
  (2 shorter events, 0.1 us)
Async XLA Ops:
  0.0 27.6 %copy-start = (bf16[256,384]{1,0:T(8,128)(2,1)S(1)}, bf16[256,384]{1,0:T(8,128)(2,1)}, u32[]{:S(2)}) copy-start(bf16[256,384]{1,0:T(8,128)(2,1)} %param.1) | copy-start | bytes 589828
  19.0 8.6 %collective-permute-start = (bf16[4,256,384]{1,2,0:T(8,128)(2,1)S(1)}, bf16[4,256,384]{1,2,0:T(8,128)(2,1)S(1)}, u32[]{:S(2)}, u32[]{:S(2)}) collective-permute-start(bf16[4,256,384]{1,2,0:T(8,128)(2,1)S(1)} %copy.7), channel_id=1, source_target_pairs={{0,1},{1,0},{2,3},{3,2},{4,5},{5,4},{6,7},{7,6},{8,9},{9,8},{10,11... | collective-permute-start | bytes 2359304 | tf_op jit(solution)/shard_map/panel/ppermute | solution.py:34
  27.6 1.0 copy-start.2
  110.3 34.9 %copy-start.3 = (bf16[4,256,384]{1,2,0:T(8,128)(2,1)S(1)}, bf16[4,256,384]{1,2,0:T(8,128)(2,1)}, u32[]{:S(2)}) copy-start(bf16[4,256,384]{1,2,0:T(8,128)(2,1)} %copy-done.2) | copy-start | bytes 2359300
  145.2 26.4 %copy-start.1 = (bf16[256,384]{1,0:T(8,128)(2,1)S(1)}, bf16[256,384]{1,0:T(8,128)(2,1)}, u32[]{:S(2)}) copy-start(bf16[256,384]{1,0:T(8,128)(2,1)} %param.1) | copy-start | bytes 589828
  162.2 9.3 %collective-permute-start.1 = (bf16[4,256,384]{2,1,0:T(8,128)(2,1)S(1)}, bf16[4,256,384]{2,1,0:T(8,128)(2,1)S(1)}, u32[]{:S(2)}, u32[]{:S(2)}) collective-permute-start(bf16[4,256,384]{2,1,0:T(8,128)(2,1)S(1)} %bitcast.26), channel_id=1, source_target_pairs={{0,1},{1,0},{2,3},{3,2},{4,5},{5,4},{6,7},{7,6},{8,9},{9,8},{10,11... | collective-permute-start | bytes 2359304 | tf_op jit(solution)/shard_map/mixed_panel/ppermute | solution.py:34

commit v3 on v1

v3 whole, which is shorter than its diff:
```python
import math

import jax
import jax.numpy as jnp
import numpy as np
from jax import lax
from jax.sharding import Mesh
from jax.sharding import PartitionSpec as P

coef_first = 3.4445
coef_middle = -4.775
coef_last = 2.0315

axes = ("yl", "z", "x", "yh", "core")
row_axes = ("yl", "z", "x")
col_axes = ("yh", "core")
axis_sizes = (2, 12, 4, 4, 2)


def grouped(key, place):
    members = {}
    for device, at in enumerate(np.ndindex(*axis_sizes)):
        members.setdefault(key(*at), []).append((place(*at), device))
    return [[device for _, device in sorted(group)] for group in members.values()]


def along_x(core):
    return grouped(
        lambda yl, z, x, yh, c: (yl, z, -1, yh, c) if c == core else (-1, z // 2, x, yh, c),
        lambda yl, z, x, yh, c: x if c == core else 2 * yl + z % 2,
    )


stages = (
    (4, along_x(0)),
    (4, along_x(1)),
    (6, grouped(lambda yl, z, x, yh, c: (yl, z % 2, x, yh, c), lambda yl, z, x, yh, c: z)),
)


def exchange(blocks, groups):
    return lax.all_to_all(blocks, axes, 0, 0, axis_index_groups=groups, tiled=True)


def add_up(parts):
    return jnp.sum(parts.astype(jnp.float32), axis=0).astype(jnp.bfloat16)


def gather_columns(block):
    near = lax.all_gather(block, "yh", axis=0)
    far = lax.ppermute(near, "core", [(0, 1), (1, 0)])
    return jnp.concatenate([near, far], axis=0)


def times(left, right):
    return lax.dot_general(
        left, right, (((0, 2), (0, 1)), ((), ())), preferred_element_type=jnp.float32
    )


def body(momentum):
    with jax.named_scope("panel"):
        panel = gather_columns(momentum)
    with jax.named_scope("gram"):
        piece = lax.dot_general(
            panel, momentum, (((1,), (0,)), ((), ())), preferred_element_type=jnp.float32
        ).astype(jnp.bfloat16)
    width = momentum.shape[1]
    with jax.named_scope("reduce"):
        for count, groups in stages:
            piece = add_up(exchange(piece.reshape(count, -1, width), groups))
    with jax.named_scope("collect"):
        for count, groups in reversed(stages):
            piece = piece.reshape(-1, width)
            piece = exchange(jnp.broadcast_to(piece[None], (count,) + piece.shape), groups)
        gram = piece.reshape(8, width, width)
    with jax.named_scope("mixed"):
        mixed = times(panel, gram).astype(jnp.bfloat16)
    with jax.named_scope("mixed_panel"):
        mixed_panel = gather_columns(mixed)
    with jax.named_scope("second"):
        second = times(mixed_panel, gram)
        rms_scale = 0.2 * math.sqrt(max(momentum.shape[0] * 96, 3072))
        total = (
            coef_first * momentum.astype(jnp.float32)
            + coef_middle * mixed.astype(jnp.float32)
            + coef_last * second
        )
        return (rms_scale * total).astype(jnp.bfloat16)


def solution(mesh):
    fine = Mesh(mesh.devices.reshape(axis_sizes), axes)
    return jax.shard_map(
        body,
        mesh=fine,
        in_specs=(P(row_axes, col_axes),),
        out_specs=P(row_axes, col_axes),
        check_vma=False,
    )
```

time: 185 us -> 158 us (0.85)
  the two profiles are of different devices: /device:TPU:65 before, /device:TPU:1 now
where the time goes in v3:
time: 158 us; the launch traced here: 157 us
  blocking collectives  128 us (81%)
  starting transfers between devices  19.9 us (13%)
  waiting for transfers between devices  3.78 us (2%)
  matrix products  3.68 us (2%)
    all_to_all x6, blocking collectives, exchange(): lax.all_to_all(blocks, axes, 0, 0, axis_index_groups=groups, tiled=True)  91.1 us
    all_gather x2, blocking collectives, gather_columns(): near = lax.all_gather(block, 'yh', axis=0)  37.3 us
    ppermute x2, starting transfers between devices, gather_columns(): far = lax.ppermute(near, 'core', [(0, 1), (1, 0)])  19.9 us
    ppermute x2, waiting for transfers between devices, gather_columns(): far = lax.ppermute(near, 'core', [(0, 1), (1, 0)])  3.78 us
  transfers between devices with their start and end apart: 2, of which 2 were waited for; matrix products, arithmetic and copies ran while one was open for 0% of the time, Pallas kernels for 0%

profile of v3, /device:TPU:1, one launch (start us, length us, event | category | flops | bytes accessed | tf_op | source)
XLA Modules:
  0.0 157.3 jit_solution(3803895707524555425)
XLA Ops:
  0.0 0.0 copy-start.2
  0.0 21.1 %all-gather = bf16[1024,384]{1,0:T(8,128)(2,1)S(1)} all-gather(bf16[256,384]{1,0:T(8,128)(2,1)} %param.1), channel_id=2, replica_groups=mesh['yl'=2,'z'=12,'x'=4,'yh'=4,'core'=2] {'yh'}, dimensions={0}, use_global_device_ids=true | all-gather | bytes 983040 | tf_op jit(solution)/shard_map/panel/all_gather | solution.py:50
  21.1 0.3 copy.7
  21.3 0.0 copy-start
  21.4 8.9 %collective-permute-start = (bf16[4,256,384]{1,2,0:T(8,128)(2,1)S(1)}, bf16[4,256,384]{1,2,0:T(8,128)(2,1)S(1)}, u32[]{:S(2)}, u32[]{:S(2)}) collective-permute-start(bf16[4,256,384]{1,2,0:T(8,128)(2,1)S(1)} %copy.7), channel_id=1, source_target_pairs={{0,1},{1,0},{2,3},{3,2},{4,5},{5,4},{6,7},{7,6},{8,9},{9,8},{10,11... | collective-permute-start | bytes 2359304 | tf_op jit(solution)/shard_map/panel/ppermute | solution.py:51
  30.3 1.9 %collective-permute-done = bf16[4,256,384]{1,2,0:T(8,128)(2,1)S(1)} collective-permute-done((bf16[4,256,384]{1,2,0:T(8,128)(2,1)S(1)}, bf16[4,256,384]{1,2,0:T(8,128)(2,1)S(1)}, u32[]{:S(2)}, u32[]{:S(2)}) %collective-permute-start) | collective-permute-done | bytes 786464 | tf_op jit(solution)/shard_map/panel/ppermute | solution.py:51
  32.2 0.0 copy-done.2
  32.2 0.0 copy-start.3
  32.2 1.0 convolution_convert_fusion
  33.2 0.0 copy-done
  33.2 0.0 copy-done.3
  33.2 18.6 %all_to_all.30 = bf16[4,768,384]{2,1,0:T(8,128)(2,1)S(1)} all-to-all(bf16[4,768,384]{2,1,0:T(8,128)(2,1)S(1)} %bitcast.30), channel_id=1, replica_groups={{0,8,16,24},{1,33,385,417},{2,10,18,26},{3,35,387,419},{4,12,20,28},{5,..., dimensions={0} | all-to-all | bytes 4718592 | tf_op jit(solution)/shard_map/reduce/all_to_all | solution.py:42
  51.8 0.7 reduce_sum.36
  52.5 9.7 %all_to_all.31 = bf16[4,192,384]{2,1,0:T(8,128)(2,1)S(1)} all-to-all(bf16[4,192,384]{2,1,0:T(8,128)(2,1)S(1)} %bitcast.31), channel_id=1, replica_groups={{0,32,384,416},{1,9,17,25},{2,34,386,418},{3,11,19,27},{4,36,388,420},{..., dimensions={0} | all-to-all | bytes 1179648 | tf_op jit(solution)/shard_map/reduce/all_to_all | solution.py:42
  62.2 0.1 reduce_sum.37
  62.3 21.7 %all_to_all.32 = bf16[6,32,384]{2,1,0:T(8,128)(2,1)S(1)} all-to-all(bf16[6,32,384]{2,1,0:T(8,128)(2,1)S(1)} %bitcast.35), channel_id=1, replica_groups={{0,64,128,192,256,320},{1,65,129,193,257,321},{2,66,130,194,258,322},{3..., dimensions={0} | all-to-all | bytes 294912 | tf_op jit(solution)/shard_map/reduce/all_to_all | solution.py:42
  84.0 12.8 %all_to_all.33 = bf16[6,32,384]{2,1,0:T(8,128)(2,1)S(1)} all-to-all(bf16[6,32,384]{2,1,0:T(8,128)(2,1)S(1)} %broadcast_in_dim.20), channel_id=1, replica_groups={{0,64,128,192,256,320},{1,65,129,193,257,321},{2,66,130,194,258,322},{3..., dimensions={0} | all-to-all | bytes 294912 | tf_op jit(solution)/shard_map/collect/all_to_all | solution.py:42
  96.8 0.1 broadcast_in_dim.22
  96.8 9.7 %all_to_all.34 = bf16[4,192,384]{2,1,0:T(8,128)(2,1)S(1)} all-to-all(bf16[4,192,384]{2,1,0:T(8,128)(2,1)S(1)} %broadcast_in_dim.22), channel_id=1, replica_groups={{0,32,384,416},{1,9,17,25},{2,34,386,418},{3,11,19,27},{4,36,388,420},{..., dimensions={0} | all-to-all | bytes 1179648 | tf_op jit(solution)/shard_map/collect/all_to_all | solution.py:42
  106.5 0.2 broadcast_in_dim.24
  106.7 0.0 copy-start.1
  106.7 0.0 copy-start.4
  106.7 18.7 %all_to_all.35 = bf16[4,768,384]{2,1,0:T(8,128)(2,1)S(1)} all-to-all(bf16[4,768,384]{2,1,0:T(8,128)(2,1)S(1)} %broadcast_in_dim.24), channel_id=1, replica_groups={{0,8,16,24},{1,33,385,417},{2,10,18,26},{3,35,387,419},{4,12,20,28},{5,..., dimensions={0} | all-to-all | bytes 4718592 | tf_op jit(solution)/shard_map/collect/all_to_all | solution.py:42
  125.4 0.0 copy-done.1
  125.4 0.0 copy-done.4
  125.4 1.0 fusion.19
  126.5 16.2 %all-gather.1 = bf16[1024,384]{1,0:T(8,128)(2,1)S(1)} all-gather(bf16[256,384]{1,0:T(8,128)(2,1)S(1)} %fusion.19), channel_id=3, replica_groups=mesh['yl'=2,'z'=12,'x'=4,'yh'=4,'core'=2] {'yh'}, dimensions={0}, use_global_device_ids=true | all-gather | bytes 983040 | tf_op jit(solution)/shard_map/mixed_panel/all_gather | solution.py:50
  142.7 11.0 %collective-permute-start.1 = (bf16[4,256,384]{2,1,0:T(8,128)(2,1)S(1)}, bf16[4,256,384]{2,1,0:T(8,128)(2,1)S(1)}, u32[]{:S(2)}, u32[]{:S(2)}) collective-permute-start(bf16[4,256,384]{2,1,0:T(8,128)(2,1)S(1)} %bitcast.33), channel_id=1, source_target_pairs={{0,1},{1,0},{2,3},{3,2},{4,5},{5,4},{6,7},{7,6},{8,9},{9,8},{10,11... | collective-permute-start | bytes 2359304 | tf_op jit(solution)/shard_map/mixed_panel/ppermute | solution.py:51
  153.7 1.9 %collective-permute-done.1 = bf16[4,256,384]{2,1,0:T(8,128)(2,1)S(1)} collective-permute-done((bf16[4,256,384]{2,1,0:T(8,128)(2,1)S(1)}, bf16[4,256,384]{2,1,0:T(8,128)(2,1)S(1)}, u32[]{:S(2)}, u32[]{:S(2)}) %collective-permute-start.1) | collective-permute-done | bytes 786464 | tf_op jit(solution)/shard_map/mixed_panel/ppermute | solution.py:51
  155.6 1.7 %fusion.16 = bf16[256,384]{1,0:T(8,128)(2,1)} fusion(bf16[8,384,384]{2,1,0:T(8,128)(2,1)S(1)} %bitcast.29, bf16[4,256,384]{2,1,0:T(8,128)(2,1)S(1)} %collective-permute-done.1, bf16[4,256,384]{2,1,0:T(8,128)(2,1)S(1)} %bitcast.34, bf16[256,384]{1,0:T(8,128)(2,1)S(1)} %fusion.19, bf16[256,384]{1,0:T(8,128)(2,1)S(1)} %copy-done.2), kind=kOutput, calls=%fused_computation.11 | convolution fusion | flops 605650944 | bytes 4521984 | tf_op jit(solution)/shard_map/second/dot_general | solution.py:56
  (2 shorter events, 0.0 us)
Async XLA Ops:
  0.0 32.2 %copy-start.2 = (bf16[256,384]{1,0:T(8,128)(2,1)S(1)}, bf16[256,384]{1,0:T(8,128)(2,1)}, u32[]{:S(2)}) copy-start(bf16[256,384]{1,0:T(8,128)(2,1)} %param.1) | copy-start | bytes 589828
  21.3 11.8 %copy-start = (bf16[4,256,384]{1,2,0:T(8,128)(2,1)}, bf16[4,256,384]{1,2,0:T(8,128)(2,1)S(1)}, u32[]{:S(2)}) copy-start(bf16[4,256,384]{1,2,0:T(8,128)(2,1)S(1)} %copy.7) | copy-start | bytes 2359300
  21.4 10.8 %collective-permute-start = (bf16[4,256,384]{1,2,0:T(8,128)(2,1)S(1)}, bf16[4,256,384]{1,2,0:T(8,128)(2,1)S(1)}, u32[]{:S(2)}, u32[]{:S(2)}) collective-permute-start(bf16[4,256,384]{1,2,0:T(8,128)(2,1)S(1)} %copy.7), channel_id=1, source_target_pairs={{0,1},{1,0},{2,3},{3,2},{4,5},{5,4},{6,7},{7,6},{8,9},{9,8},{10,11... | collective-permute-start | bytes 2359304 | tf_op jit(solution)/shard_map/panel/ppermute | solution.py:51
  32.2 1.0 copy-start.3
  106.7 18.7 %copy-start.1 = (bf16[4,256,384]{1,2,0:T(8,128)(2,1)S(1)}, bf16[4,256,384]{1,2,0:T(8,128)(2,1)}, u32[]{:S(2)}) copy-start(bf16[4,256,384]{1,2,0:T(8,128)(2,1)} %copy-done) | copy-start | bytes 2359300
  106.7 18.7 %copy-start.4 = (bf16[4,256,384]{1,2,0:T(8,128)(2,1)S(1)}, bf16[4,256,384]{1,2,0:T(8,128)(2,1)}, u32[]{:S(2)}) copy-start(bf16[4,256,384]{1,2,0:T(8,128)(2,1)} %copy-done.3) | copy-start | bytes 2359300
  142.7 12.9 %collective-permute-start.1 = (bf16[4,256,384]{2,1,0:T(8,128)(2,1)S(1)}, bf16[4,256,384]{2,1,0:T(8,128)(2,1)S(1)}, u32[]{:S(2)}, u32[]{:S(2)}) collective-permute-start(bf16[4,256,384]{2,1,0:T(8,128)(2,1)S(1)} %bitcast.33), channel_id=1, source_target_pairs={{0,1},{1,0},{2,3},{3,2},{4,5},{5,4},{6,7},{7,6},{8,9},{9,8},{10,11... | collective-permute-start | bytes 2359304 | tf_op jit(solution)/shard_map/mixed_panel/ppermute | solution.py:51

commit v4 on v3

--- a/solution.py
+++ b/solution.py
@@ -38,12 +38,18 @@
 )
 
 
+wide = grouped(
+    lambda yl, z, x, yh, c: (-1, z // 2, -1, yh, c),
+    lambda yl, z, x, yh, c: 4 * x + 2 * yl + z % 2 if c == 0 else 4 * (2 * yl + z % 2) + x,
+)
+
+
 def exchange(blocks, groups):
     return lax.all_to_all(blocks, axes, 0, 0, axis_index_groups=groups, tiled=True)
 
 
 def add_up(parts):
-    return jnp.sum(parts.astype(jnp.float32), axis=0).astype(jnp.bfloat16)
+    return sum(parts[i].astype(jnp.float32) for i in range(parts.shape[0])).astype(jnp.bfloat16)
 
 
 def gather_columns(block):
@@ -70,7 +76,7 @@
         for count, groups in stages:
             piece = add_up(exchange(piece.reshape(count, -1, width), groups))
     with jax.named_scope("collect"):
-        for count, groups in reversed(stages):
+        for count, groups in (stages[2], (16, wide)):
             piece = piece.reshape(-1, width)
             piece = exchange(jnp.broadcast_to(piece[None], (count,) + piece.shape), groups)
         gram = piece.reshape(8, width, width)

time: 158 us -> 155 us (0.981)
    all_to_all x6 -> x5, blocking collectives: 91.1 us -> 90.2 us  [exchange(): lax.all_to_all(blocks, axes, 0, 0, axis_index_groups=groups, tiled=True)]
where the time goes in v4:
time: 155 us
  blocking collectives  127 us (82%)
  starting transfers between devices  19.1 us (12%)
  waiting for transfers between devices  3.78 us (2%)
  matrix products  3.7 us (2%)
    all_to_all x5, blocking collectives, exchange(): lax.all_to_all(blocks, axes, 0, 0, axis_index_groups=groups, tiled=True)  90.2 us
    all_gather x2, blocking collectives, gather_columns(): near = lax.all_gather(block, 'yh', axis=0)  37 us
    ppermute x2, starting transfers between devices, gather_columns(): far = lax.ppermute(near, 'core', [(0, 1), (1, 0)])  19.1 us
    ppermute x2, waiting for transfers between devices, gather_columns(): far = lax.ppermute(near, 'core', [(0, 1), (1, 0)])  3.78 us
  transfers between devices with their start and end apart: 2, of which 2 were waited for; matrix products, arithmetic and copies ran while one was open for 0% of the time, Pallas kernels for 0%

profile of v4, /device:TPU:1, one launch (start us, length us, event | category | flops | bytes accessed | tf_op | source)
XLA Modules:
  0.0 154.8 jit_solution(1124168818712056568)
XLA Ops:
  0.0 0.0 copy-start
  0.0 21.1 %all-gather = bf16[1024,384]{1,0:T(8,128)(2,1)S(1)} all-gather(bf16[256,384]{1,0:T(8,128)(2,1)} %param.1), channel_id=2, replica_groups=mesh['yl'=2,'z'=12,'x'=4,'yh'=4,'core'=2] {'yh'}, dimensions={0}, use_global_device_ids=true | all-gather | bytes 983040 | tf_op jit(solution)/shard_map/panel/all_gather | solution.py:56
  21.1 0.3 copy.4
  21.3 8.9 %collective-permute-start = (bf16[4,256,384]{1,2,0:T(8,128)(2,1)S(1)}, bf16[4,256,384]{1,2,0:T(8,128)(2,1)S(1)}, u32[]{:S(2)}, u32[]{:S(2)}) collective-permute-start(bf16[4,256,384]{1,2,0:T(8,128)(2,1)S(1)} %copy.4), channel_id=1, source_target_pairs={{0,1},{1,0},{2,3},{3,2},{4,5},{5,4},{6,7},{7,6},{8,9},{9,8},{10,11... | collective-permute-start | bytes 2359304 | tf_op jit(solution)/shard_map/panel/ppermute | solution.py:57
  30.3 1.9 %collective-permute-done = bf16[4,256,384]{1,2,0:T(8,128)(2,1)S(1)} collective-permute-done((bf16[4,256,384]{1,2,0:T(8,128)(2,1)S(1)}, bf16[4,256,384]{1,2,0:T(8,128)(2,1)S(1)}, u32[]{:S(2)}, u32[]{:S(2)}) %collective-permute-start) | collective-permute-done | bytes 786464 | tf_op jit(solution)/shard_map/panel/ppermute | solution.py:57
  32.2 0.0 copy-done
  32.2 1.0 convolution_convert_fusion
  33.1 18.6 %all_to_all.25 = bf16[4,768,384]{2,1,0:T(8,128)(2,1)S(1)} all-to-all(bf16[4,768,384]{2,1,0:T(8,128)(2,1)S(1)} %bitcast.31), channel_id=1, replica_groups={{0,8,16,24},{1,33,385,417},{2,10,18,26},{3,35,387,419},{4,12,20,28},{5,..., dimensions={0} | all-to-all | bytes 4718592 | tf_op jit(solution)/shard_map/reduce/all_to_all | solution.py:48
  51.7 0.3 add_convert_fusion
  52.0 9.7 %all_to_all.26 = bf16[4,192,384]{2,1,0:T(8,128)(2,1)S(1)} all-to-all(bf16[4,192,384]{2,1,0:T(8,128)(2,1)S(1)} %bitcast.32), channel_id=1, replica_groups={{0,32,384,416},{1,9,17,25},{2,34,386,418},{3,11,19,27},{4,36,388,420},{..., dimensions={0} | all-to-all | bytes 1179648 | tf_op jit(solution)/shard_map/reduce/all_to_all | solution.py:48
  61.7 0.1 add_convert_fusion.1
  61.8 21.7 %all_to_all.27 = bf16[6,32,384]{2,1,0:T(8,128)(2,1)S(1)} all-to-all(bf16[6,32,384]{2,1,0:T(8,128)(2,1)S(1)} %bitcast.36), channel_id=1, replica_groups={{0,64,128,192,256,320},{1,65,129,193,257,321},{2,66,130,194,258,322},{3..., dimensions={0} | all-to-all | bytes 294912 | tf_op jit(solution)/shard_map/reduce/all_to_all | solution.py:48
  83.5 12.8 %all_to_all.28 = bf16[6,32,384]{2,1,0:T(8,128)(2,1)S(1)} all-to-all(bf16[6,32,384]{2,1,0:T(8,128)(2,1)S(1)} %broadcast_in_dim.16), channel_id=1, replica_groups={{0,64,128,192,256,320},{1,65,129,193,257,321},{2,66,130,194,258,322},{3..., dimensions={0} | all-to-all | bytes 294912 | tf_op jit(solution)/shard_map/collect/all_to_all | solution.py:48
  96.3 0.3 broadcast_in_dim.18
  96.6 27.5 %all_to_all.29 = bf16[16,192,384]{2,1,0:T(8,128)(2,1)S(1)} all-to-all(bf16[16,192,384]{2,1,0:T(8,128)(2,1)S(1)} %broadcast_in_dim.18), channel_id=1, replica_groups={{0,32,384,416,8,40,392,424,16,48,400,432,24,56,408,440},{1,9,17,25,33,4..., dimensions={0} | all-to-all | bytes 4718592 | tf_op jit(solution)/shard_map/collect/all_to_all | solution.py:48
  124.1 1.0 fusion.19
  125.1 15.9 %all-gather.1 = bf16[1024,384]{1,0:T(8,128)(2,1)S(1)} all-gather(bf16[256,384]{1,0:T(8,128)(2,1)S(1)} %fusion.19), channel_id=3, replica_groups=mesh['yl'=2,'z'=12,'x'=4,'yh'=4,'core'=2] {'yh'}, dimensions={0}, use_global_device_ids=true | all-gather | bytes 983040 | tf_op jit(solution)/shard_map/mixed_panel/all_gather | solution.py:56
  141.0 10.2 %collective-permute-start.1 = (bf16[4,256,384]{2,1,0:T(8,128)(2,1)S(1)}, bf16[4,256,384]{2,1,0:T(8,128)(2,1)S(1)}, u32[]{:S(2)}, u32[]{:S(2)}) collective-permute-start(bf16[4,256,384]{2,1,0:T(8,128)(2,1)S(1)} %bitcast.33), channel_id=1, source_target_pairs={{0,1},{1,0},{2,3},{3,2},{4,5},{5,4},{6,7},{7,6},{8,9},{9,8},{10,11... | collective-permute-start | bytes 2359304 | tf_op jit(solution)/shard_map/mixed_panel/ppermute | solution.py:57
  151.2 1.9 %collective-permute-done.1 = bf16[4,256,384]{2,1,0:T(8,128)(2,1)S(1)} collective-permute-done((bf16[4,256,384]{2,1,0:T(8,128)(2,1)S(1)}, bf16[4,256,384]{2,1,0:T(8,128)(2,1)S(1)}, u32[]{:S(2)}, u32[]{:S(2)}) %collective-permute-start.1) | collective-permute-done | bytes 786464 | tf_op jit(solution)/shard_map/mixed_panel/ppermute | solution.py:57
  153.1 1.7 %fusion.16 = bf16[256,384]{1,0:T(8,128)(2,1)} fusion(bf16[8,384,384]{2,1,0:T(8,128)(2,1)S(1)} %bitcast.30, bf16[4,256,384]{2,1,0:T(8,128)(2,1)S(1)} %collective-permute-done.1, bf16[4,256,384]{2,1,0:T(8,128)(2,1)S(1)} %bitcast.34, bf16[256,384]{1,0:T(8,128)(2,1)S(1)} %fusion.19, bf16[256,384]{1,0:T(8,128)(2,1)S(1)} %copy-done), kind=kOutput, calls=%fused_computation.12 | convolution fusion | flops 605650944 | bytes 4521984 | tf_op jit(solution)/shard_map/second/dot_general | solution.py:62
  (2 shorter events, 0.0 us)
Async XLA Ops:
  0.0 32.2 %copy-start = (bf16[256,384]{1,0:T(8,128)(2,1)S(1)}, bf16[256,384]{1,0:T(8,128)(2,1)}, u32[]{:S(2)}) copy-start(bf16[256,384]{1,0:T(8,128)(2,1)} %param.1) | copy-start | bytes 589828
  21.3 10.8 %collective-permute-start = (bf16[4,256,384]{1,2,0:T(8,128)(2,1)S(1)}, bf16[4,256,384]{1,2,0:T(8,128)(2,1)S(1)}, u32[]{:S(2)}, u32[]{:S(2)}) collective-permute-start(bf16[4,256,384]{1,2,0:T(8,128)(2,1)S(1)} %copy.4), channel_id=1, source_target_pairs={{0,1},{1,0},{2,3},{3,2},{4,5},{5,4},{6,7},{7,6},{8,9},{9,8},{10,11... | collective-permute-start | bytes 2359304 | tf_op jit(solution)/shard_map/panel/ppermute | solution.py:57
  141.0 12.1 %collective-permute-start.1 = (bf16[4,256,384]{2,1,0:T(8,128)(2,1)S(1)}, bf16[4,256,384]{2,1,0:T(8,128)(2,1)S(1)}, u32[]{:S(2)}, u32[]{:S(2)}) collective-permute-start(bf16[4,256,384]{2,1,0:T(8,128)(2,1)S(1)} %bitcast.33), channel_id=1, source_target_pairs={{0,1},{1,0},{2,3},{3,2},{4,5},{5,4},{6,7},{7,6},{8,9},{9,8},{10,11... | collective-permute-start | bytes 2359304 | tf_op jit(solution)/shard_map/mixed_panel/ppermute | solution.py:57

commit v5 on v4

--- a/solution.py
+++ b/solution.py
@@ -15,6 +15,7 @@
 row_axes = ("yl", "z", "x")
 col_axes = ("yh", "core")
 axis_sizes = (2, 12, 4, 4, 2)
+around = (0, 2, 1, 3)
 
 
 def grouped(key, place):
@@ -27,20 +28,20 @@
 def along_x(core):
     return grouped(
         lambda yl, z, x, yh, c: (yl, z, -1, yh, c) if c == core else (-1, z // 2, x, yh, c),
-        lambda yl, z, x, yh, c: x if c == core else 2 * yl + z % 2,
+        lambda yl, z, x, yh, c: around[x] if c == core else 2 * yl + z % 2,
     )
 
 
 stages = (
+    (4, along_x(1)),
     (4, along_x(0)),
-    (4, along_x(1)),
     (6, grouped(lambda yl, z, x, yh, c: (yl, z % 2, x, yh, c), lambda yl, z, x, yh, c: z)),
 )
 
 
 wide = grouped(
     lambda yl, z, x, yh, c: (-1, z // 2, -1, yh, c),
-    lambda yl, z, x, yh, c: 4 * x + 2 * yl + z % 2 if c == 0 else 4 * (2 * yl + z % 2) + x,
+    lambda yl, z, x, yh, c: 4 * around[x] + 2 * yl + z % 2 if c == 1 else 4 * (2 * yl + z % 2) + around[x],
 )
 
 
@@ -55,7 +56,7 @@
 def gather_columns(block):
     near = lax.all_gather(block, "yh", axis=0)
     far = lax.ppermute(near, "core", [(0, 1), (1, 0)])
-    return jnp.concatenate([near, far], axis=0)
+    return near, far
 
 
 def times(left, right):
@@ -66,7 +67,7 @@
 
 def body(momentum):
     with jax.named_scope("panel"):
-        panel = gather_columns(momentum)
+        panel = jnp.concatenate(gather_columns(momentum), axis=0)
     with jax.named_scope("gram"):
         piece = lax.dot_general(
             panel, momentum, (((1,), (0,)), ((), ())), preferred_element_type=jnp.float32
@@ -83,9 +84,9 @@
     with jax.named_scope("mixed"):
         mixed = times(panel, gram).astype(jnp.bfloat16)
     with jax.named_scope("mixed_panel"):
-        mixed_panel = gather_columns(mixed)
+        near, far = gather_columns(mixed)
     with jax.named_scope("second"):
-        second = times(mixed_panel, gram)
+        second = times(near, gram[:4]) + times(far, gram[4:])
         rms_scale = 0.2 * math.sqrt(max(momentum.shape[0] * 96, 3072))
         total = (
             coef_first * momentum.astype(jnp.float32)

time: 155 us -> 154 us (level)
  blocking collectives: 127 us -> 125 us
  starting transfers between devices: 19.1 us -> 20.8 us
    ppermute x2, starting transfers between devices: 19.1 us -> 20.8 us  [gather_columns(): far = lax.ppermute(near, 'core', [(0, 1), (1, 0)])]
  transfers between devices with their start and end apart: 2 -> 2, of which waited for: 2 -> 2; matrix products, arithmetic and copies ran while one was open for 0% -> 1% of each run, Pallas kernels for 0% -> 0%
where the time goes in v5:
time: 154 us
  blocking collectives  125 us (81%)
  starting transfers between devices  20.8 us (14%)
  matrix products  3.84 us (2%)
  waiting for transfers between devices  2.95 us (2%)
    all_to_all x5, blocking collectives, exchange(): lax.all_to_all(blocks, axes, 0, 0, axis_index_groups=groups, tiled=True)  89 us
    all_gather x2, blocking collectives, gather_columns(): near = lax.all_gather(block, 'yh', axis=0)  36.3 us
    ppermute x2, starting transfers between devices, gather_columns(): far = lax.ppermute(near, 'core', [(0, 1), (1, 0)])  20.8 us
  transfers between devices with their start and end apart: 2, of which 2 were waited for; matrix products, arithmetic and copies ran while one was open for 1% of the time, Pallas kernels for 0%

profile of v5, /device:TPU:1, one launch (start us, length us, event | category | flops | bytes accessed | tf_op | source)
XLA Modules:
  0.0 154.1 jit_solution(2764461844677849931)
XLA Ops:
  0.0 0.0 copy-start
  0.0 21.1 %all-gather = bf16[1024,384]{1,0:T(8,128)(2,1)S(1)} all-gather(bf16[256,384]{1,0:T(8,128)(2,1)} %param.1), channel_id=2, replica_groups=mesh['yl'=2,'z'=12,'x'=4,'yh'=4,'core'=2] {'yh'}, dimensions={0}, use_global_device_ids=true | all-gather | bytes 983040 | tf_op jit(solution)/shard_map/panel/all_gather | solution.py:57
  21.1 0.3 copy.4
  21.3 8.9 %collective-permute-start = (bf16[4,256,384]{1,2,0:T(8,128)(2,1)S(1)}, bf16[4,256,384]{1,2,0:T(8,128)(2,1)S(1)}, u32[]{:S(2)}, u32[]{:S(2)}) collective-permute-start(bf16[4,256,384]{1,2,0:T(8,128)(2,1)S(1)} %copy.4), channel_id=1, source_target_pairs={{0,1},{1,0},{2,3},{3,2},{4,5},{5,4},{6,7},{7,6},{8,9},{9,8},{10,11... | collective-permute-start | bytes 2359304 | tf_op jit(solution)/shard_map/panel/ppermute | solution.py:58
  30.3 1.9 %collective-permute-done = bf16[4,256,384]{1,2,0:T(8,128)(2,1)S(1)} collective-permute-done((bf16[4,256,384]{1,2,0:T(8,128)(2,1)S(1)}, bf16[4,256,384]{1,2,0:T(8,128)(2,1)S(1)}, u32[]{:S(2)}, u32[]{:S(2)}) %collective-permute-start) | collective-permute-done | bytes 786464 | tf_op jit(solution)/shard_map/panel/ppermute | solution.py:58
  32.2 0.0 copy-done
  32.2 1.0 convolution_convert_fusion
  33.1 19.1 %all_to_all.25 = bf16[4,768,384]{2,1,0:T(8,128)(2,1)S(1)} all-to-all(bf16[4,768,384]{2,1,0:T(8,128)(2,1)S(1)} %bitcast.42), channel_id=1, replica_groups={{0,32,384,416},{1,17,9,25},{2,34,386,418},{3,19,11,27},{4,36,388,420},{..., dimensions={0} | all-to-all | bytes 4718592 | tf_op jit(solution)/shard_map/reduce/all_to_all | solution.py:49
  52.2 0.3 add_convert_fusion
  52.5 9.2 %all_to_all.26 = bf16[4,192,384]{2,1,0:T(8,128)(2,1)S(1)} all-to-all(bf16[4,192,384]{2,1,0:T(8,128)(2,1)S(1)} %bitcast.43), channel_id=1, replica_groups={{0,16,8,24},{1,33,385,417},{2,18,10,26},{3,35,387,419},{4,20,12,28},{5,..., dimensions={0} | all-to-all | bytes 1179648 | tf_op jit(solution)/shard_map/reduce/all_to_all | solution.py:49
  61.7 0.1 add_convert_fusion.1
  61.8 21.6 %all_to_all.27 = bf16[6,32,384]{2,1,0:T(8,128)(2,1)S(1)} all-to-all(bf16[6,32,384]{2,1,0:T(8,128)(2,1)S(1)} %bitcast.46), channel_id=1, replica_groups={{0,64,128,192,256,320},{1,65,129,193,257,321},{2,66,130,194,258,322},{3..., dimensions={0} | all-to-all | bytes 294912 | tf_op jit(solution)/shard_map/reduce/all_to_all | solution.py:49
  83.4 12.8 %all_to_all.28 = bf16[6,32,384]{2,1,0:T(8,128)(2,1)S(1)} all-to-all(bf16[6,32,384]{2,1,0:T(8,128)(2,1)S(1)} %broadcast_in_dim.16), channel_id=1, replica_groups={{0,64,128,192,256,320},{1,65,129,193,257,321},{2,66,130,194,258,322},{3..., dimensions={0} | all-to-all | bytes 294912 | tf_op jit(solution)/shard_map/collect/all_to_all | solution.py:49
  96.3 0.3 broadcast_in_dim.18
  96.6 26.3 %all_to_all.29 = bf16[16,192,384]{2,1,0:T(8,128)(2,1)S(1)} all-to-all(bf16[16,192,384]{2,1,0:T(8,128)(2,1)S(1)} %broadcast_in_dim.18), channel_id=1, replica_groups={{0,16,8,24,32,48,40,56,384,400,392,408,416,432,424,440},{1,33,385,417,1..., dimensions={0} | all-to-all | bytes 4718592 | tf_op jit(solution)/shard_map/collect/all_to_all | solution.py:49
  122.9 1.0 fusion.5
  123.9 15.2 %all-gather.1 = bf16[1024,384]{1,0:T(8,128)(2,1)S(1)} all-gather(bf16[256,384]{1,0:T(8,128)(2,1)S(1)} %fusion.5), channel_id=3, replica_groups=mesh['yl'=2,'z'=12,'x'=4,'yh'=4,'core'=2] {'yh'}, dimensions={0}, use_global_device_ids=true | all-gather | bytes 983040 | tf_op jit(solution)/shard_map/mixed_panel/all_gather | solution.py:57
  139.1 11.8 %collective-permute-start.1 = (bf16[4,256,384]{2,1,0:T(8,128)(2,1)S(1)}, bf16[4,256,384]{2,1,0:T(8,128)(2,1)S(1)}, u32[]{:S(2)}, u32[]{:S(2)}) collective-permute-start(bf16[4,256,384]{2,1,0:T(8,128)(2,1)S(1)} %bitcast.40), channel_id=1, source_target_pairs={{0,1},{1,0},{2,3},{3,2},{4,5},{5,4},{6,7},{7,6},{8,9},{9,8},{10,11... | collective-permute-start | bytes 2359304 | tf_op jit(solution)/shard_map/mixed_panel/ppermute | solution.py:58
  151.0 0.2 fusion.10
  151.2 0.6 convolution_bitcast_fusion.1
  151.8 1.1 collective-permute-done.1
  152.9 1.3 fusion.4
  (2 shorter events, 0.0 us)
Async XLA Ops:
  0.0 32.2 %copy-start = (bf16[256,384]{1,0:T(8,128)(2,1)S(1)}, bf16[256,384]{1,0:T(8,128)(2,1)}, u32[]{:S(2)}) copy-start(bf16[256,384]{1,0:T(8,128)(2,1)} %param.1) | copy-start | bytes 589828
  21.3 10.8 %collective-permute-start = (bf16[4,256,384]{1,2,0:T(8,128)(2,1)S(1)}, bf16[4,256,384]{1,2,0:T(8,128)(2,1)S(1)}, u32[]{:S(2)}, u32[]{:S(2)}) collective-permute-start(bf16[4,256,384]{1,2,0:T(8,128)(2,1)S(1)} %copy.4), channel_id=1, source_target_pairs={{0,1},{1,0},{2,3},{3,2},{4,5},{5,4},{6,7},{7,6},{8,9},{9,8},{10,11... | collective-permute-start | bytes 2359304 | tf_op jit(solution)/shard_map/panel/ppermute | solution.py:58
  139.1 13.7 %collective-permute-start.1 = (bf16[4,256,384]{2,1,0:T(8,128)(2,1)S(1)}, bf16[4,256,384]{2,1,0:T(8,128)(2,1)S(1)}, u32[]{:S(2)}, u32[]{:S(2)}) collective-permute-start(bf16[4,256,384]{2,1,0:T(8,128)(2,1)S(1)} %bitcast.40), channel_id=1, source_target_pairs={{0,1},{1,0},{2,3},{3,2},{4,5},{5,4},{6,7},{7,6},{8,9},{9,8},{10,11... | collective-permute-start | bytes 2359304 | tf_op jit(solution)/shard_map/mixed_panel/ppermute | solution.py:58

commit v6 on v5

--- a/solution.py
+++ b/solution.py
@@ -15,7 +15,7 @@
 row_axes = ("yl", "z", "x")
 col_axes = ("yh", "core")
 axis_sizes = (2, 12, 4, 4, 2)
-around = (0, 2, 1, 3)
+around = (0, 1, 3, 2)
 
 
 def grouped(key, place):
@@ -86,13 +86,13 @@
     with jax.named_scope("mixed_panel"):
         near, far = gather_columns(mixed)
     with jax.named_scope("second"):
-        second = times(near, gram[:4]) + times(far, gram[4:])
         rms_scale = 0.2 * math.sqrt(max(momentum.shape[0] * 96, 3072))
-        total = (
+        started = (
             coef_first * momentum.astype(jnp.float32)
             + coef_middle * mixed.astype(jnp.float32)
-            + coef_last * second
+            + coef_last * times(near, gram[:4])
         )
+        total = started + coef_last * times(far, gram[4:])
         return (rms_scale * total).astype(jnp.bfloat16)
 
 

time: 154 us -> 154 us (level)
  no operation moved by 1% of the time
where the time goes in v6:
time: 154 us; the launch traced here: 153 us
  blocking collectives  125 us (81%)
  starting transfers between devices  20 us (13%)
  matrix products  3.84 us (2%)
  waiting for transfers between devices  2.94 us (2%)
    all_to_all x5, blocking collectives, exchange(): lax.all_to_all(blocks, axes, 0, 0, axis_index_groups=groups, tiled=True)  87.6 us
    all_gather x2, blocking collectives, gather_columns(): near = lax.all_gather(block, 'yh', axis=0)  37.7 us
    ppermute x2, starting transfers between devices, gather_columns(): far = lax.ppermute(near, 'core', [(0, 1), (1, 0)])  20 us
  transfers between devices with their start and end apart: 2, of which 2 were waited for; matrix products, arithmetic and copies ran while one was open for 1% of the time, Pallas kernels for 0%

profile of v6, /device:TPU:1, one launch (start us, length us, event | category | flops | bytes accessed | tf_op | source)
XLA Modules:
  0.0 153.4 jit_solution(6014306840106560801)
XLA Ops:
  0.0 0.0 copy-start
  0.0 21.1 %all-gather = bf16[1024,384]{1,0:T(8,128)(2,1)S(1)} all-gather(bf16[256,384]{1,0:T(8,128)(2,1)} %param.1), channel_id=2, replica_groups=mesh['yl'=2,'z'=12,'x'=4,'yh'=4,'core'=2] {'yh'}, dimensions={0}, use_global_device_ids=true | all-gather | bytes 983040 | tf_op jit(solution)/shard_map/panel/all_gather | solution.py:57
  21.1 0.3 copy.4
  21.3 8.9 %collective-permute-start = (bf16[4,256,384]{1,2,0:T(8,128)(2,1)S(1)}, bf16[4,256,384]{1,2,0:T(8,128)(2,1)S(1)}, u32[]{:S(2)}, u32[]{:S(2)}) collective-permute-start(bf16[4,256,384]{1,2,0:T(8,128)(2,1)S(1)} %copy.4), channel_id=1, source_target_pairs={{0,1},{1,0},{2,3},{3,2},{4,5},{5,4},{6,7},{7,6},{8,9},{9,8},{10,11... | collective-permute-start | bytes 2359304 | tf_op jit(solution)/shard_map/panel/ppermute | solution.py:58
  30.3 1.9 %collective-permute-done = bf16[4,256,384]{1,2,0:T(8,128)(2,1)S(1)} collective-permute-done((bf16[4,256,384]{1,2,0:T(8,128)(2,1)S(1)}, bf16[4,256,384]{1,2,0:T(8,128)(2,1)S(1)}, u32[]{:S(2)}, u32[]{:S(2)}) %collective-permute-start) | collective-permute-done | bytes 786464 | tf_op jit(solution)/shard_map/panel/ppermute | solution.py:58
  32.2 0.0 copy-done
  32.2 1.0 convolution_convert_fusion
  33.1 19.1 %all_to_all.25 = bf16[4,768,384]{2,1,0:T(8,128)(2,1)S(1)} all-to-all(bf16[4,768,384]{2,1,0:T(8,128)(2,1)S(1)} %bitcast.42), channel_id=1, replica_groups={{0,32,384,416},{1,9,25,17},{2,34,386,418},{3,11,27,19},{4,36,388,420},{..., dimensions={0} | all-to-all | bytes 4718592 | tf_op jit(solution)/shard_map/reduce/all_to_all | solution.py:49
  52.2 0.3 add_convert_fusion
  52.5 9.2 %all_to_all.26 = bf16[4,192,384]{2,1,0:T(8,128)(2,1)S(1)} all-to-all(bf16[4,192,384]{2,1,0:T(8,128)(2,1)S(1)} %bitcast.43), channel_id=1, replica_groups={{0,8,24,16},{1,33,385,417},{2,10,26,18},{3,35,387,419},{4,12,28,20},{5,..., dimensions={0} | all-to-all | bytes 1179648 | tf_op jit(solution)/shard_map/reduce/all_to_all | solution.py:49
  61.7 0.1 add_convert_fusion.1
  61.8 21.6 %all_to_all.27 = bf16[6,32,384]{2,1,0:T(8,128)(2,1)S(1)} all-to-all(bf16[6,32,384]{2,1,0:T(8,128)(2,1)S(1)} %bitcast.48), channel_id=1, replica_groups={{0,64,128,192,256,320},{1,65,129,193,257,321},{2,66,130,194,258,322},{3..., dimensions={0} | all-to-all | bytes 294912 | tf_op jit(solution)/shard_map/reduce/all_to_all | solution.py:49
  83.4 12.8 %all_to_all.28 = bf16[6,32,384]{2,1,0:T(8,128)(2,1)S(1)} all-to-all(bf16[6,32,384]{2,1,0:T(8,128)(2,1)S(1)} %broadcast_in_dim.16), channel_id=1, replica_groups={{0,64,128,192,256,320},{1,65,129,193,257,321},{2,66,130,194,258,322},{3..., dimensions={0} | all-to-all | bytes 294912 | tf_op jit(solution)/shard_map/collect/all_to_all | solution.py:49
  96.3 0.3 broadcast_in_dim.18
  96.6 24.9 %all_to_all.29 = bf16[16,192,384]{2,1,0:T(8,128)(2,1)S(1)} all-to-all(bf16[16,192,384]{2,1,0:T(8,128)(2,1)S(1)} %broadcast_in_dim.18), channel_id=1, replica_groups={{0,8,24,16,32,40,56,48,384,392,408,400,416,424,440,432},{1,33,385,417,9..., dimensions={0} | all-to-all | bytes 4718592 | tf_op jit(solution)/shard_map/collect/all_to_all | solution.py:49
  121.5 1.0 fusion.6
  122.5 16.6 %all-gather.1 = bf16[1024,384]{1,0:T(8,128)(2,1)S(1)} all-gather(bf16[256,384]{1,0:T(8,128)(2,1)S(1)} %fusion.6), channel_id=3, replica_groups=mesh['yl'=2,'z'=12,'x'=4,'yh'=4,'core'=2] {'yh'}, dimensions={0}, use_global_device_ids=true | all-gather | bytes 983040 | tf_op jit(solution)/shard_map/mixed_panel/all_gather | solution.py:57
  139.1 11.1 %collective-permute-start.1 = (bf16[4,256,384]{2,1,0:T(8,128)(2,1)S(1)}, bf16[4,256,384]{2,1,0:T(8,128)(2,1)S(1)}, u32[]{:S(2)}, u32[]{:S(2)}) collective-permute-start(bf16[4,256,384]{2,1,0:T(8,128)(2,1)S(1)} %bitcast.45), channel_id=1, source_target_pairs={{0,1},{1,0},{2,3},{3,2},{4,5},{5,4},{6,7},{7,6},{8,9},{9,8},{10,11... | collective-permute-start | bytes 2359304 | tf_op jit(solution)/shard_map/mixed_panel/ppermute | solution.py:58
  150.3 0.2 fusion.11
  150.5 0.6 fusion.1
  151.1 1.1 collective-permute-done.1
  152.1 1.3 fusion.5
  (2 shorter events, 0.0 us)
Async XLA Ops:
  0.0 32.2 %copy-start = (bf16[256,384]{1,0:T(8,128)(2,1)S(1)}, bf16[256,384]{1,0:T(8,128)(2,1)}, u32[]{:S(2)}) copy-start(bf16[256,384]{1,0:T(8,128)(2,1)} %param.1) | copy-start | bytes 589828
  21.3 10.8 %collective-permute-start = (bf16[4,256,384]{1,2,0:T(8,128)(2,1)S(1)}, bf16[4,256,384]{1,2,0:T(8,128)(2,1)S(1)}, u32[]{:S(2)}, u32[]{:S(2)}) collective-permute-start(bf16[4,256,384]{1,2,0:T(8,128)(2,1)S(1)} %copy.4), channel_id=1, source_target_pairs={{0,1},{1,0},{2,3},{3,2},{4,5},{5,4},{6,7},{7,6},{8,9},{9,8},{10,11... | collective-permute-start | bytes 2359304 | tf_op jit(solution)/shard_map/panel/ppermute | solution.py:58
  139.1 13.0 %collective-permute-start.1 = (bf16[4,256,384]{2,1,0:T(8,128)(2,1)S(1)}, bf16[4,256,384]{2,1,0:T(8,128)(2,1)S(1)}, u32[]{:S(2)}, u32[]{:S(2)}) collective-permute-start(bf16[4,256,384]{2,1,0:T(8,128)(2,1)S(1)} %bitcast.45), channel_id=1, source_target_pairs={{0,1},{1,0},{2,3},{3,2},{4,5},{5,4},{6,7},{7,6},{8,9},{9,8},{10,11... | collective-permute-start | bytes 2359304 | tf_op jit(solution)/shard_map/mixed_panel/ppermute | solution.py:58

commit v7 on v6

--- a/solution.py
+++ b/solution.py
@@ -15,7 +15,7 @@
 row_axes = ("yl", "z", "x")
 col_axes = ("yh", "core")
 axis_sizes = (2, 12, 4, 4, 2)
-around = (0, 1, 3, 2)
+around = ((0, 1, 3, 2), (0, 2, 3, 1))
 
 
 def grouped(key, place):
@@ -28,7 +28,7 @@
 def along_x(core):
     return grouped(
         lambda yl, z, x, yh, c: (yl, z, -1, yh, c) if c == core else (-1, z // 2, x, yh, c),
-        lambda yl, z, x, yh, c: around[x] if c == core else 2 * yl + z % 2,
+        lambda yl, z, x, yh, c: around[c][x] if c == core else 2 * yl + z % 2,
     )
 
 
@@ -41,7 +41,7 @@
 
 wide = grouped(
     lambda yl, z, x, yh, c: (-1, z // 2, -1, yh, c),
-    lambda yl, z, x, yh, c: 4 * around[x] + 2 * yl + z % 2 if c == 1 else 4 * (2 * yl + z % 2) + around[x],
+    lambda yl, z, x, yh, c: 4 * around[c][x] + 2 * yl + z % 2 if c == 1 else 4 * (2 * yl + z % 2) + around[c][x],
 )
 
 

time: 154 us -> 155 us (level)
  starting transfers between devices: 20 us -> 21.6 us
    ppermute x2, starting transfers between devices: 20 us -> 21.6 us  [gather_columns(): far = lax.ppermute(near, 'core', [(0, 1), (1, 0)])]
where the time goes in v7:
time: 155 us
  blocking collectives  125 us (81%)
  starting transfers between devices  21.6 us (14%)
  matrix products  3.84 us (2%)
  waiting for transfers between devices  2.94 us (2%)
    all_to_all x5, blocking collectives, exchange(): lax.all_to_all(blocks, axes, 0, 0, axis_index_groups=groups, tiled=True)  88.7 us
    all_gather x2, blocking collectives, gather_columns(): near = lax.all_gather(block, 'yh', axis=0)  36.2 us
    ppermute x2, starting transfers between devices, gather_columns(): far = lax.ppermute(near, 'core', [(0, 1), (1, 0)])  21.6 us
  transfers between devices with their start and end apart: 2, of which 2 were waited for; matrix products, arithmetic and copies ran while one was open for 1% of the time, Pallas kernels for 0%

profile of v7, /device:TPU:1, one launch (start us, length us, event | category | flops | bytes accessed | tf_op | source)
XLA Modules:
  0.0 154.6 jit_solution(8276721139698605073)
XLA Ops:
  0.0 0.0 copy-start
  0.0 21.1 %all-gather = bf16[1024,384]{1,0:T(8,128)(2,1)S(1)} all-gather(bf16[256,384]{1,0:T(8,128)(2,1)} %param.1), channel_id=2, replica_groups=mesh['yl'=2,'z'=12,'x'=4,'yh'=4,'core'=2] {'yh'}, dimensions={0}, use_global_device_ids=true | all-gather | bytes 983040 | tf_op jit(solution)/shard_map/panel/all_gather | solution.py:57
  21.1 0.3 copy.4
  21.3 8.9 %collective-permute-start = (bf16[4,256,384]{1,2,0:T(8,128)(2,1)S(1)}, bf16[4,256,384]{1,2,0:T(8,128)(2,1)S(1)}, u32[]{:S(2)}, u32[]{:S(2)}) collective-permute-start(bf16[4,256,384]{1,2,0:T(8,128)(2,1)S(1)} %copy.4), channel_id=1, source_target_pairs={{0,1},{1,0},{2,3},{3,2},{4,5},{5,4},{6,7},{7,6},{8,9},{9,8},{10,11... | collective-permute-start | bytes 2359304 | tf_op jit(solution)/shard_map/panel/ppermute | solution.py:58
  30.3 1.9 %collective-permute-done = bf16[4,256,384]{1,2,0:T(8,128)(2,1)S(1)} collective-permute-done((bf16[4,256,384]{1,2,0:T(8,128)(2,1)S(1)}, bf16[4,256,384]{1,2,0:T(8,128)(2,1)S(1)}, u32[]{:S(2)}, u32[]{:S(2)}) %collective-permute-start) | collective-permute-done | bytes 786464 | tf_op jit(solution)/shard_map/panel/ppermute | solution.py:58
  32.2 0.0 copy-done
  32.2 1.0 convolution_convert_fusion
  33.1 19.1 %all_to_all.25 = bf16[4,768,384]{2,1,0:T(8,128)(2,1)S(1)} all-to-all(bf16[4,768,384]{2,1,0:T(8,128)(2,1)S(1)} %bitcast.42), channel_id=1, replica_groups={{0,32,384,416},{1,25,9,17},{2,34,386,418},{3,27,11,19},{4,36,388,420},{..., dimensions={0} | all-to-all | bytes 4718592 | tf_op jit(solution)/shard_map/reduce/all_to_all | solution.py:49
  52.2 0.3 add_convert_fusion
  52.5 9.2 %all_to_all.26 = bf16[4,192,384]{2,1,0:T(8,128)(2,1)S(1)} all-to-all(bf16[4,192,384]{2,1,0:T(8,128)(2,1)S(1)} %bitcast.43), channel_id=1, replica_groups={{0,8,24,16},{1,33,385,417},{2,10,26,18},{3,35,387,419},{4,12,28,20},{5,..., dimensions={0} | all-to-all | bytes 1179648 | tf_op jit(solution)/shard_map/reduce/all_to_all | solution.py:49
  61.7 0.1 add_convert_fusion.1
  61.8 21.6 %all_to_all.27 = bf16[6,32,384]{2,1,0:T(8,128)(2,1)S(1)} all-to-all(bf16[6,32,384]{2,1,0:T(8,128)(2,1)S(1)} %bitcast.48), channel_id=1, replica_groups={{0,64,128,192,256,320},{1,65,129,193,257,321},{2,66,130,194,258,322},{3..., dimensions={0} | all-to-all | bytes 294912 | tf_op jit(solution)/shard_map/reduce/all_to_all | solution.py:49
  83.4 12.8 %all_to_all.28 = bf16[6,32,384]{2,1,0:T(8,128)(2,1)S(1)} all-to-all(bf16[6,32,384]{2,1,0:T(8,128)(2,1)S(1)} %broadcast_in_dim.16), channel_id=1, replica_groups={{0,64,128,192,256,320},{1,65,129,193,257,321},{2,66,130,194,258,322},{3..., dimensions={0} | all-to-all | bytes 294912 | tf_op jit(solution)/shard_map/collect/all_to_all | solution.py:49
  96.3 0.3 broadcast_in_dim.18
  96.6 26.0 %all_to_all.29 = bf16[16,192,384]{2,1,0:T(8,128)(2,1)S(1)} all-to-all(bf16[16,192,384]{2,1,0:T(8,128)(2,1)S(1)} %broadcast_in_dim.18), channel_id=1, replica_groups={{0,8,24,16,32,40,56,48,384,392,408,400,416,424,440,432},{1,33,385,417,2..., dimensions={0} | all-to-all | bytes 4718592 | tf_op jit(solution)/shard_map/collect/all_to_all | solution.py:49
  122.6 1.0 fusion.6
  123.6 15.2 %all-gather.1 = bf16[1024,384]{1,0:T(8,128)(2,1)S(1)} all-gather(bf16[256,384]{1,0:T(8,128)(2,1)S(1)} %fusion.6), channel_id=3, replica_groups=mesh['yl'=2,'z'=12,'x'=4,'yh'=4,'core'=2] {'yh'}, dimensions={0}, use_global_device_ids=true | all-gather | bytes 983040 | tf_op jit(solution)/shard_map/mixed_panel/all_gather | solution.py:57
  138.8 12.7 %collective-permute-start.1 = (bf16[4,256,384]{2,1,0:T(8,128)(2,1)S(1)}, bf16[4,256,384]{2,1,0:T(8,128)(2,1)S(1)}, u32[]{:S(2)}, u32[]{:S(2)}) collective-permute-start(bf16[4,256,384]{2,1,0:T(8,128)(2,1)S(1)} %bitcast.45), channel_id=1, source_target_pairs={{0,1},{1,0},{2,3},{3,2},{4,5},{5,4},{6,7},{7,6},{8,9},{9,8},{10,11... | collective-permute-start | bytes 2359304 | tf_op jit(solution)/shard_map/mixed_panel/ppermute | solution.py:58
  151.5 0.2 fusion.11
  151.7 0.6 fusion.1
  152.3 1.1 collective-permute-done.1
  153.4 1.3 fusion.5
  (2 shorter events, 0.0 us)
Async XLA Ops:
  0.0 32.2 %copy-start = (bf16[256,384]{1,0:T(8,128)(2,1)S(1)}, bf16[256,384]{1,0:T(8,128)(2,1)}, u32[]{:S(2)}) copy-start(bf16[256,384]{1,0:T(8,128)(2,1)} %param.1) | copy-start | bytes 589828
  21.3 10.8 %collective-permute-start = (bf16[4,256,384]{1,2,0:T(8,128)(2,1)S(1)}, bf16[4,256,384]{1,2,0:T(8,128)(2,1)S(1)}, u32[]{:S(2)}, u32[]{:S(2)}) collective-permute-start(bf16[4,256,384]{1,2,0:T(8,128)(2,1)S(1)} %copy.4), channel_id=1, source_target_pairs={{0,1},{1,0},{2,3},{3,2},{4,5},{5,4},{6,7},{7,6},{8,9},{9,8},{10,11... | collective-permute-start | bytes 2359304 | tf_op jit(solution)/shard_map/panel/ppermute | solution.py:58
  138.8 14.6 %collective-permute-start.1 = (bf16[4,256,384]{2,1,0:T(8,128)(2,1)S(1)}, bf16[4,256,384]{2,1,0:T(8,128)(2,1)S(1)}, u32[]{:S(2)}, u32[]{:S(2)}) collective-permute-start(bf16[4,256,384]{2,1,0:T(8,128)(2,1)S(1)} %bitcast.45), channel_id=1, source_target_pairs={{0,1},{1,0},{2,3},{3,2},{4,5},{5,4},{6,7},{7,6},{8,9},{9,8},{10,11... | collective-permute-start | bytes 2359304 | tf_op jit(solution)/shard_map/mixed_panel/ppermute | solution.py:58
